TPU v7x, 32 devices: a whole 2x2x4 slice. The times are simulated.
32 devices in a mesh: rep: 2 (over y), pool: 16 (over z, x, core).
Axes of the slice: x: 2, y: 2, z: 4, core: 2. Of those that a mesh axis runs over, the one named last changes fastest.
Arguments:
- pool_kv: bfloat16 [128, 8, 16, 256], P(('rep', 'pool')), parts along dimension 0, may hold values from -6 to 6
- prefix_table: int32 [4, 32], P('rep'), parts along dimension 0, may hold values from 0 to 63, as said below
- prefix_count: int32 [4], P('rep'), parts along dimension 0, may hold values from 17 to 32, as said below
- prefill_q: bfloat16 [32, 512, 1024], P(('rep', 'pool')), parts along dimension 0, may hold values from -25 to 25
- prefill_new_kv: bfloat16 [32, 512, 256], P(('rep', 'pool')), parts along dimension 0, may hold values from -6 to 6
- decode_q: bfloat16 [512, 8192], P(('rep', 'pool')), parts along dimension 0, may hold values from -25 to 25
- decode_new: bfloat16 [512, 2048], P(('rep', 'pool')), parts along dimension 0, may hold values from -6 to 6
- decode_cache: bfloat16 [32, 128, 2, 64, 256], P(('rep', 'pool')), parts along dimension 0, may hold values from -6 to 6
- decode_group: int32 [512, 1], P('rep'), parts along dimension 0, may hold values from 0 to 3; in each aligned block of 16 rows (0 to 15, 16 to 31, ...) at most 8 rows name the same one
- cached_len: int32 [512], P('rep'), parts along dimension 0, may hold values from 1 to 64, 8192 in all
Outputs:
- prefill_out: bfloat16 [32, 512, 1024], P(('rep', 'pool')), parts along dimension 0
- decode_out: bfloat16 [512, 8192], P(('rep', 'pool')), parts along dimension 0
There are 2 independent parts, one for each index of `rep`. A program takes and returns all parts, laid end to end along the dimension named above; each array names one. Nothing has to cross between parts.
Inputs may be any that keep to these rules, and one draw needn't show every extreme that they name: prefix_table[g, j] = o * 4 + b names block b of owner o. No block appears twice in the table. Among the first prefix_count[g] entries of a row, every owner holds at most 2; entries from prefix_count[g] on are not read. `prefix_count`: at least one request has 32 blocks. `decode_group`: among the rows of one home device, no group is named by more than 8 rows.
All inputs are finite; a program needn't handle non-finite values.
Results may differ from a plain program's by a relative error of at most 0.0055.
Values may be sent and summed in bfloat16 or wider, within the bound.
No kernel may reach another device: no remote copies, remote signals or barrier semaphores. Data moves between devices by JAX's collectives and lax.ppermute only.
A program may use at most 128 MiB of HBM per device.

v0:
```python
import jax
import jax.numpy as jnp
from jax import lax
from jax.sharding import PartitionSpec as P

QPK = 8
PGRP = 8
DGRP = 4
PCAP = 2


MASKED = -1e30


def prefix_send(pool_kv, prefix_table, prefix_count, device):
    blocks_here = pool_kv.shape[0]
    head_count = pool_kv.shape[1]
    group_count, most_blocks = prefix_table.shape
    owner_ids = prefix_table // blocks_here
    listed = jnp.arange(most_blocks)[None, :] < prefix_count[:, None]
    owned_here = (owner_ids == device) & listed
    block_rank = jnp.cumsum(owned_here.astype(jnp.int32), axis=1) - 1
    chosen = owned_here[:, :, None] & (block_rank[:, :, None] == jnp.arange(PCAP)[None, None, :])
    local_ids = (prefix_table - device * blocks_here)[:, :, None]
    slot_ids = jnp.sum(jnp.where(chosen, local_ids, 0), axis=1)
    slot_index = jnp.broadcast_to(slot_ids[:, None, :], (group_count, head_count, PCAP))
    head_index = jnp.broadcast_to(
        jnp.arange(head_count)[None, :, None], (group_count, head_count, PCAP)
    )
    outgoing = pool_kv[slot_index, head_index]
    return outgoing.reshape((group_count * head_count,) + outgoing.shape[2:])


def prefix_valid(prefix_table, prefix_count, blocks_here, device_count, group_id):
    table_row = prefix_table[group_id]
    listed = jnp.arange(table_row.shape[0]) < prefix_count[group_id]
    owner_ids = table_row // blocks_here
    per_source = jnp.sum(
        ((owner_ids[None, :] == jnp.arange(device_count)[:, None]) & listed[None, :]).astype(
            jnp.int32
        ),
        axis=1,
    )
    return per_source[:, None] > jnp.arange(PCAP)[None, :]


def prefill_attend(queries, new_kv, arrived, block_live):
    token_count = queries.shape[0]
    head_dim = new_kv.shape[1] // 2
    prefix_keys = arrived[..., :head_dim].reshape(-1, head_dim)
    prefix_values = arrived[..., head_dim:].reshape(-1, head_dim)
    prefix_live = jnp.broadcast_to(block_live[:, :, None], arrived.shape[:3]).reshape(-1)
    token_pos = jnp.arange(token_count)
    causal = token_pos[:, None] >= token_pos[None, :]
    score_scale = head_dim ** (-0.5)
    head_blocks = queries.reshape(token_count, 2, -1, head_dim).transpose(1, 0, 2, 3)

    def one_block(block_queries):
        cached_scores = (
            jnp.einsum(
                "thd,kd->htk", block_queries, prefix_keys, preferred_element_type=jnp.float32
            )
            * score_scale
        )
        cached_scores = jnp.where(prefix_live[None, None, :], cached_scores, MASKED)
        fresh_scores = (
            jnp.einsum(
                "thd,sd->hts",
                block_queries,
                new_kv[:, :head_dim],
                preferred_element_type=jnp.float32,
            )
            * score_scale
        )
        fresh_scores = jnp.where(causal[None, :, :], fresh_scores, MASKED)
        highest = jnp.maximum(jnp.max(cached_scores, axis=-1), jnp.max(fresh_scores, axis=-1))[
            ..., None
        ]
        cached_exp = jnp.where(prefix_live[None, None, :], jnp.exp(cached_scores - highest), 0.0)
        fresh_exp = jnp.where(causal[None, :, :], jnp.exp(fresh_scores - highest), 0.0)
        denominator = jnp.sum(cached_exp, axis=-1, keepdims=True) + jnp.sum(
            fresh_exp, axis=-1, keepdims=True
        )
        cached_weights = (cached_exp / denominator).astype(jnp.bfloat16)
        fresh_weights = (fresh_exp / denominator).astype(jnp.bfloat16)
        mixed = jnp.einsum(
            "htk,kd->thd", cached_weights, prefix_values, preferred_element_type=jnp.float32
        )
        mixed = mixed + jnp.einsum(
            "hts,sd->thd", fresh_weights, new_kv[:, head_dim:], preferred_element_type=jnp.float32
        )
        return mixed.astype(jnp.bfloat16)

    blocks_out = lax.map(one_block, head_blocks)
    return blocks_out.transpose(1, 0, 2, 3).reshape(token_count, -1)


def decode_attend(received, cache_slots, slot_lengths):
    slot_total, pair_count, position_count, double_dim = cache_slots.shape
    head_dim = double_dim // 2
    query_width = pair_count * QPK * head_dim
    queries = received[:, :query_width].reshape(slot_total, pair_count, QPK, head_dim)
    own_kv = received[:, query_width:].reshape(slot_total, pair_count, double_dim)
    score_scale = head_dim ** (-0.5)
    position_live = (jnp.arange(position_count)[None, :] < slot_lengths[:, None])[:, None, None, :]
    cached_scores = (
        jnp.einsum(
            "skqd,sktd->skqt",
            queries,
            cache_slots[..., :head_dim],
            preferred_element_type=jnp.float32,
        )
        * score_scale
    )
    cached_scores = jnp.where(position_live, cached_scores, MASKED)
    own_scores = (
        jnp.einsum(
            "skqd,skd->skq", queries, own_kv[..., :head_dim], preferred_element_type=jnp.float32
        )
        * score_scale
    )
    highest = jnp.maximum(jnp.max(cached_scores, axis=-1), own_scores)
    cached_exp = jnp.where(position_live, jnp.exp(cached_scores - highest[..., None]), 0.0)
    own_exp = jnp.exp(own_scores - highest)
    denominator = jnp.sum(cached_exp, axis=-1) + own_exp
    cached_weights = (cached_exp / denominator[..., None]).astype(jnp.bfloat16)
    own_weights = (own_exp / denominator).astype(jnp.bfloat16)
    mixed = jnp.einsum(
        "skqt,sktd->skqd",
        cached_weights,
        cache_slots[..., head_dim:],
        preferred_element_type=jnp.float32,
    )
    mixed = mixed + own_weights.astype(jnp.float32)[..., None] * own_kv[
        :, :, None, head_dim:
    ].astype(jnp.float32)
    return mixed.reshape(slot_total, -1).astype(jnp.bfloat16)


def shards(
    pool_kv,
    prefix_table,
    prefix_count,
    prefill_q,
    prefill_new_kv,
    decode_q,
    decode_new,
    decode_cache,
    decode_group,
    cached_len,
):
    device = lax.axis_index("pool")
    device_count = lax.axis_size("pool")
    outgoing = prefix_send(pool_kv, prefix_table, prefix_count, device)
    arrived = lax.all_to_all(outgoing, "pool", split_axis=0, concat_axis=0, tiled=True)
    block_live = prefix_valid(
        prefix_table, prefix_count, pool_kv.shape[0], device_count, device // PGRP
    )
    prefill_out = prefill_attend(prefill_q[0], prefill_new_kv[0], arrived, block_live)
    row_count = decode_q.shape[0]
    slot_cap = decode_cache.shape[1] // device_count
    group_count = device_count // DGRP
    all_groups = decode_group[:, 0]
    home_groups = lax.dynamic_slice_in_dim(all_groups, device * row_count, row_count)
    home_match = home_groups[:, None] == jnp.arange(group_count)[None, :]
    home_rank = jnp.sum(
        jnp.where(home_match, jnp.cumsum(home_match.astype(jnp.int32), axis=0) - 1, 0), axis=1
    )
    chosen = home_match[:, :, None] & (
        home_rank[:, None, None] == jnp.arange(slot_cap)[None, None, :]
    )
    row_for = jnp.sum(jnp.where(chosen, jnp.arange(row_count)[:, None, None], 0), axis=0)
    payload = jnp.concatenate(
        [decode_q.reshape(row_count, DGRP, -1), decode_new.reshape(row_count, DGRP, -1)], axis=2
    )
    row_index = jnp.broadcast_to(row_for[:, None, :], (group_count, DGRP, slot_cap))
    member_index = jnp.broadcast_to(jnp.arange(DGRP)[None, :, None], (group_count, DGRP, slot_cap))
    sending = payload[row_index, member_index].reshape(device_count, slot_cap, -1)
    received = lax.all_to_all(sending, "pool", split_axis=0, concat_axis=0, tiled=True)
    group_id = device // DGRP
    table_groups = all_groups.reshape(device_count, row_count)
    table_match = table_groups == group_id
    table_rank = jnp.cumsum(table_match.astype(jnp.int32), axis=1) - 1
    slot_pick = table_match[:, :, None] & (
        table_rank[:, :, None] == jnp.arange(slot_cap)[None, None, :]
    )
    global_rows = jnp.arange(device_count)[:, None] * row_count + jnp.arange(row_count)[None, :]
    row_ids = jnp.sum(jnp.where(slot_pick, global_rows[:, :, None], 0), axis=1)
    slot_live = jnp.any(slot_pick, axis=1)
    slot_lengths = jnp.where(slot_live, cached_len[row_ids], 0).reshape(-1)
    answers = decode_attend(
        received.reshape(device_count * slot_cap, -1), decode_cache[0], slot_lengths
    )
    returned = lax.all_to_all(
        answers.reshape(device_count, slot_cap, -1), "pool", split_axis=0, concat_axis=0, tiled=True
    )
    back_rows = home_groups[:, None] * DGRP + jnp.arange(DGRP)[None, :]
    back_slots = jnp.broadcast_to(home_rank[:, None], (row_count, DGRP))
    decode_out = returned[back_rows, back_slots].reshape(row_count, -1)
    return (prefill_out[None], decode_out)


def solution(mesh):
    in_specs = (
        P(("rep", "pool"), None, None, None),
        P("rep", None),
        P("rep"),
        P(("rep", "pool"), None, None),
        P(("rep", "pool"), None, None),
        P(("rep", "pool"), None),
        P(("rep", "pool"), None),
        P(("rep", "pool"), None, None, None, None),
        P("rep", None),
        P("rep"),
    )
    out_specs = (P(("rep", "pool"), None, None), P(("rep", "pool"), None))
    return jax.shard_map(shards, mesh=mesh, in_specs=in_specs, out_specs=out_specs, check_vma=False)
```

profile of v0, /device:TPU:0, one launch (start us, length us, event | category | flops | bytes accessed | tf_op | source)
XLA Modules:
  0.0 88.5 jit_solution(10865689429348576502)
XLA Ops:
  0.7 0.8 fusion.73
  1.5 0.2 reduce_window_sum.33
  1.7 0.7 broadcast_subtract_fusion
  2.6 1.3 %gather_fusion = bf16[32,16,256]{2,1,0:T(8,128)(2,1)} fusion(bf16[4,8,16,256]{3,2,1,0:T(8,128)(2,1)S(1)} %copy-done, s32[32]{0:T(128)S(1)} %reshape.342), kind=kCustom, calls=%fused_computation | custom fusion | bytes 524544 | tf_op jit(solution)/shard_map/gather | solution.py:30
  4.0 7.4 %all-to-all-start = ((bf16[16,2,16,256]{3,2,1,0:T(8,128)(2,1)}), bf16[16,2,16,256]{3,2,1,0:T(8,128)(2,1)S(1)}, u32[]{:S(2)}, u32[]{:S(2)}) async-start(bf16[16,2,16,256]{3,2,1,0:T(8,128)(2,1)} %bitcast.2), calls=%async_computation | async-start | bytes 524288 | tf_op jit(solution)/shard_map/all_to_all | solution.py:155
  11.3 0.7 multiply_bitcast_fusion
  12.2 0.2 select_reduce_fusion.2
  12.7 0.9 reshape.336
  13.5 1.1 %reshape.335 = bf16[16,4,2048]{2,1,0:T(4,128)(2,1)S(1)} reshape(bf16[16,8192]{1,0:T(8,128)(2,1)} %param.17) | data formatting | bytes 524288 | tf_op jit(solution)/shard_map/reshape | solution.py:174
  14.7 0.7 compare_reduce_fusion
  15.5 0.2 reduce_window_sum.34
  15.7 0.4 fusion.60
  16.1 0.4 select_reduce_fusion
  16.8 1.3 %gather_fusion.1 = s32[128]{0:T(128)S(1)} fusion(s32[256]{0:T(256)S(1)} %copy-done.1, s32[1024]{0:T(1024)S(1)} %pad_clamp_fusion), kind=kCustom, calls=%fused_computation.1 | custom fusion | bytes 1536 | tf_op jit(solution)/shard_map/gather | solution.py:190
  18.3 0.5 copy.44
  18.9 0.6 dynamic_slice.16
  19.7 3.6 %gather_fusion.2 = bf16[128,2560]{1,0:T(8,128)(2,1)} fusion(bf16[16,4,2560]{2,1,0:T(4,128)(2,1)S(1)} %pad_maximum_fusion, s32[128]{0:T(128)S(1)} %reshape.356), kind=kCustom, calls=%fused_computation.2 | custom fusion | bytes 1311744 | tf_op jit(solution)/shard_map/gather | solution.py:178
  23.4 6.0 %all-to-all-start.1 = ((bf16[16,8,2560]{2,1,0:T(8,128)(2,1)}), bf16[16,8,2560]{2,1,0:T(8,128)(2,1)S(1)}, u32[]{:S(2)}, u32[]{:S(2)}) async-start(bf16[16,8,2560]{2,1,0:T(8,128)(2,1)} %bitcast.11), calls=%async_computation.1 | async-start | bytes 1310720 | tf_op jit(solution)/shard_map/all_to_all | solution.py:179
  29.6 0.6 iota_compare_fusion.7
  30.5 0.7 fusion.74
  31.2 14.8 %all-to-all-done.1 = bf16[16,8,2560]{2,1,0:T(8,128)(2,1)S(1)} async-done(((bf16[16,8,2560]{2,1,0:T(8,128)(2,1)}), bf16[16,8,2560]{2,1,0:T(8,128)(2,1)S(1)}, u32[]{:S(2)}, u32[]{:S(2)}) %all-to-all-start.1) | async-done | bytes 655392 | tf_op jit(solution)/shard_map/all_to_all | solution.py:179
  46.2 0.7 slice_bitcast_fusion.1
  46.9 4.6 %fusion.75 = (f32[128,2,8]{2,1,0:T(2,128)S(1)}, f32[128,2,8,64]{3,2,1,0:T(8,128)S(1)}) fusion(bf16[128,2,8,128]{3,2,1,0:T(8,128)(2,1)S(1)} %bitcast.149, bf16[128,2,64,256]{3,2,1,0:T(8,128)(2,1)} %bitcast.151, pred[128,64]{1,0:T(8,128)(4,1)S(1)} %iota_compare_fusion.2), kind=kOutput, calls=%fused_computation.128 | convolution fusion | flops 33945600 | bytes 5259264 | tf_op jit(solution)/shard_map/skqd,sktd->skqt/dot_general | solution.py:107
  51.6 0.4 fusion.57
  52.1 0.2 copy.51
  52.3 0.8 fusion.52
  53.2 0.8 copy.54
  54.0 0.8 copy.53
  54.8 3.6 %fusion.49 = bf16[128,2,8,128]{3,2,1,0:T(8,128)(2,1)S(1)} fusion(bf16[128,2,64,256]{3,2,1,0:T(8,128)(2,1)} %bitcast.152, f32[128,2,8,64]{3,2,1,0:T(8,128)S(1)} %get-tuple-element.147, f32[128,2,128]{2,1,0:T(2,128)} %get-tuple-element.139, f32[128,2,8]{2,1,0:T(2,128)} %copy.54, f32[128,2,8]{2,1,0:T(2,128)} %copy.53, f32[128,2,8]{2,1,0:T(2,128)S(1)} %copy.51, ...), kind=kOutput, calls=%fused_computation.54 | convolution fusion | flops 34865152 | bytes 5652480 | tf_op jit(solution)/shard_map/skqt,sktd->skqd/dot_general | solution.py:128
  58.4 1.0 %convert_element_type.57 = bf16[16,8,2048]{2,1,0:T(8,128)(2,1)} reshape(bf16[128,2,8,128]{3,2,1,0:T(8,128)(2,1)S(1)} %fusion.49) | data formatting | bytes 1048576 | tf_op jit(solution)/shard_map/convert_element_type | solution.py:137
  59.4 4.8 %all-to-all-start.2 = ((bf16[16,8,2048]{2,1,0:T(8,128)(2,1)}), bf16[16,8,2048]{2,1,0:T(8,128)(2,1)S(1)}, u32[]{:S(2)}, u32[]{:S(2)}) async-start(bf16[16,8,2048]{2,1,0:T(8,128)(2,1)} %convert_element_type.57), calls=%async_computation.2 | async-start | bytes 1048576 | tf_op jit(solution)/shard_map/all_to_all | solution.py:194
  64.2 18.3 %while.12 = (s32[]{:T(128)}, bf16[2,512,4,128]{3,1,2,0:T(8,128)(2,1)}, bf16[2,512,4,128]{1,3,2,0:T(8,128)(2,1)S(1)}, bf16[512,128]{1,0:T(8,128)(2,1)S(1)}, bf16[...) while((s32[]{:T(128)}, ...), condition=%wide.region_8.9_spmd.clone.clone, body=%wide.region_3.8_spmd.clone.clone.sunk | while | flops 1103884288 | bytes 39709916 | solution.py:94
  64.4 0.8 bitcast_reduce_fusion.4
  65.2 0.9 bitcast_reduce_fusion.5
  66.1 2.4 %fusion.85 = (f32[4,512]{1,0:T(4,128)S(1)}, f32[4,512]{1,0:T(4,128)S(1)}) fusion(f32[512,4,512]{0,2,1:T(8,128)S(1)} %get-tuple-element.202, f32[4,512]{1,0:T(4,128)S(1)} %max.19, pred[512,512]{0,1:T(8,128)(4,1)S(1)} %iota_compare_fusion.9, f32[512,4,512]{0,2,1:T(8,128)S(1)} %get-tuple-element.201, pred[512]{0:T(512)(128)(4,1)S(1)} %broadcast_in_dim.373), kind=kLoop, calls=%fused_computation.19.clone.1 | loop fusion | flops 10481664 | bytes 8675840 | tf_op jit(solution)/shard_map/while/body/eval_jaxpr/reduce_sum | solution.py:81
  68.6 1.7 %fusion.86 = f32[4,512,128]{2,1,0:T(8,128)S(1)} fusion(f32[512,4,512]{0,2,1:T(8,128)S(1)} %get-tuple-element.201, f32[4,512]{1,0:T(4,128)S(1)} %add.200, f32[4,512]{1,0:T(4,128)S(1)} %max.19, pred[512]{0:T(512)(128)(4,1)S(1)} %broadcast_in_dim.373, bf16[512,128]{1,0:T(8,128)(2,1)S(1)} %copy-done.6), kind=kOutput, calls=%fused_computation.20.clone.1 | convolution fusion | flops 274726912 | bytes 5390848 | tf_op jit(solution)/shard_map/while/body/eval_jaxpr/htk,kd->thd/dot_general | solution.py:86
  70.2 2.2 %fusion.87 = bf16[2,512,4,128]{3,1,2,0:T(8,128)(2,1)S(1)} fusion(bf16[2,512,4,128]{3,1,2,0:T(8,128)(2,1)S(1)} %copy-done.4, s32[]{:T(128)S(6)} %copy.66, f32[4,512,128]{2,1,0:T(8,128)S(1)} %fusion.86, f32[512,4,512]{0,2,1:T(8,128)S(1)} %get-tuple-element.202, f32[4,512]{1,0:T(4,128)S(1)} %add.200, f32[4,512]{1,0:T(4,128)S(1)} %max.19, ...), kind=kOutput, calls=%fused_computation.25.clone.1 | convolution fusion | flops 275251200 | bytes 6438916 | tf_op jit(solution)/shard_map/while/body/eval_jaxpr/hts,sd->thd/dot_general | solution.py:89
  72.4 1.0 %copy-done.5 = bf16[2,512,4,128]{3,1,2,0:T(8,128)(2,1)} copy-done((bf16[2,512,4,128]{3,1,2,0:T(8,128)(2,1)}, bf16[2,512,4,128]{3,1,2,0:T(8,128)(2,1)S(1)}, u32[]{:S(2)}) %copy-start.5) | copy-done | bytes 1048600 | tf_op jit(solution)/shard_map/while
  73.5 0.8 bitcast_reduce_fusion.4
  74.4 0.9 bitcast_reduce_fusion.5
  75.3 2.4 %fusion.85 = (f32[4,512]{1,0:T(4,128)S(1)}, f32[4,512]{1,0:T(4,128)S(1)}) fusion(f32[512,4,512]{0,2,1:T(8,128)S(1)} %get-tuple-element.202, f32[4,512]{1,0:T(4,128)S(1)} %max.19, pred[512,512]{0,1:T(8,128)(4,1)S(1)} %iota_compare_fusion.9, f32[512,4,512]{0,2,1:T(8,128)S(1)} %get-tuple-element.201, pred[512]{0:T(512)(128)(4,1)S(1)} %broadcast_in_dim.373), kind=kLoop, calls=%fused_computation.19.clone.1 | loop fusion | flops 10481664 | bytes 8675840 | tf_op jit(solution)/shard_map/while/body/eval_jaxpr/reduce_sum | solution.py:81
  77.7 1.6 %fusion.86 = f32[4,512,128]{2,1,0:T(8,128)S(1)} fusion(f32[512,4,512]{0,2,1:T(8,128)S(1)} %get-tuple-element.201, f32[4,512]{1,0:T(4,128)S(1)} %add.200, f32[4,512]{1,0:T(4,128)S(1)} %max.19, pred[512]{0:T(512)(128)(4,1)S(1)} %broadcast_in_dim.373, bf16[512,128]{1,0:T(8,128)(2,1)S(1)} %copy-done.6), kind=kOutput, calls=%fused_computation.20.clone.1 | convolution fusion | flops 274726912 | bytes 5390848 | tf_op jit(solution)/shard_map/while/body/eval_jaxpr/htk,kd->thd/dot_general | solution.py:86
  79.4 2.2 %fusion.87 = bf16[2,512,4,128]{3,1,2,0:T(8,128)(2,1)S(1)} fusion(bf16[2,512,4,128]{3,1,2,0:T(8,128)(2,1)S(1)} %copy-done.4, s32[]{:T(128)S(6)} %copy.66, f32[4,512,128]{2,1,0:T(8,128)S(1)} %fusion.86, f32[512,4,512]{0,2,1:T(8,128)S(1)} %get-tuple-element.202, f32[4,512]{1,0:T(4,128)S(1)} %add.200, f32[4,512]{1,0:T(4,128)S(1)} %max.19, ...), kind=kOutput, calls=%fused_computation.25.clone.1 | convolution fusion | flops 275251200 | bytes 6438916 | tf_op jit(solution)/shard_map/while/body/eval_jaxpr/hts,sd->thd/dot_general | solution.py:89
  81.6 1.0 %copy-done.5 = bf16[2,512,4,128]{3,1,2,0:T(8,128)(2,1)} copy-done((bf16[2,512,4,128]{3,1,2,0:T(8,128)(2,1)}, bf16[2,512,4,128]{3,1,2,0:T(8,128)(2,1)S(1)}, u32[]{:S(2)}) %copy-start.5) | copy-done | bytes 1048600 | tf_op jit(solution)/shard_map/while
  82.5 2.0 %copy.46 = bf16[512,2,4,128]{3,2,1,0:T(4,128)(2,1)S(1)} copy(bf16[512,2,4,128]{3,0,2,1:T(8,128)(2,1)} %bitcast.154) | data formatting | bytes 2097152 | tf_op jit(solution)/shard_map/transpose | solution.py:95
  84.6 1.5 %broadcast_in_dim_reshape.4 = bf16[1,512,1024]{2,1,0:T(8,128)(2,1)} reshape(bf16[512,2,4,128]{3,2,1,0:T(4,128)(2,1)S(1)} %copy.46) | data formatting | bytes 2097152 | tf_op jit(solution)/shard_map/broadcast_in_dim;reshape | solution.py:200
  86.1 1.5 %gather_fusion.3 = bf16[64,2048]{1,0:T(8,128)(2,1)S(1)} fusion(bf16[16,8,2048]{2,1,0:T(8,128)(2,1)S(1)} %all-to-all-done.2, s32[64]{0:T(128)S(1)} %reshape.362), kind=kCustom, calls=%fused_computation.3 | custom fusion | bytes 524800 | tf_op jit(solution)/shard_map/gather | solution.py:199
  87.6 0.9 %reshape.341 = bf16[16,8192]{1,0:T(8,128)(2,1)} reshape(bf16[64,2048]{1,0:T(8,128)(2,1)S(1)} %gather_fusion.3) | data formatting | bytes 524288 | tf_op jit(solution)/shard_map/reshape | solution.py:199
  (79 shorter events, 3.0 us)
Async XLA Ops:
  0.6 2.0 %copy-start = (bf16[4,8,16,256]{3,2,1,0:T(8,128)(2,1)S(1)}, bf16[4,8,16,256]{3,2,1,0:T(8,128)(2,1)}, u32[]{:S(2)}) copy-start(bf16[4,8,16,256]{3,2,1,0:T(8,128)(2,1)} %param.12) | copy-start | bytes 786436
  0.6 16.1 %copy-start.1 = (s32[256]{0:T(256)S(1)}, s32[256]{0:T(256)}, u32[]{:S(2)}) copy-start(s32[256]{0:T(256)} %param.21) | copy-start | bytes 3076
  4.0 19.4 %all-to-all-start = ((bf16[16,2,16,256]{3,2,1,0:T(8,128)(2,1)}), bf16[16,2,16,256]{3,2,1,0:T(8,128)(2,1)S(1)}, u32[]{:S(2)}, u32[]{:S(2)}) async-start(bf16[16,2,16,256]{3,2,1,0:T(8,128)(2,1)} %bitcast.2), calls=%async_computation | async-start | bytes 524288 | tf_op jit(solution)/shard_map/all_to_all | solution.py:155
  16.7 1.6 %copy-start.3 = (bf16[1,512,1024]{2,1,0:T(8,128)(2,1)S(1)}, bf16[1,512,1024]{2,1,0:T(8,128)(2,1)}, u32[]{:S(2)}) copy-start(bf16[1,512,1024]{2,1,0:T(8,128)(2,1)} %param.15) | copy-start | bytes 3145732
  16.7 2.2 %copy-start.8 = (s32[2]{0:T(128)S(1)}, s32[2]{0:T(128)}, u32[]{:S(2)}) copy-start(s32[2]{0:T(128)} %param.14) | copy-start | bytes 28
  18.3 11.2 %copy-start.7 = (s32[2,32]{1,0:T(2,128)S(1)}, s32[2,32]{1,0:T(2,128)}, u32[]{:S(2)}) copy-start(s32[2,32]{1,0:T(2,128)} %param.13) | copy-start | bytes 772
  23.4 22.6 %all-to-all-start.1 = ((bf16[16,8,2560]{2,1,0:T(8,128)(2,1)}), bf16[16,8,2560]{2,1,0:T(8,128)(2,1)S(1)}, u32[]{:S(2)}, u32[]{:S(2)}) async-start(bf16[16,8,2560]{2,1,0:T(8,128)(2,1)} %bitcast.11), calls=%async_computation.1 | async-start | bytes 1310720 | tf_op jit(solution)/shard_map/all_to_all | solution.py:179
  54.8 9.4 %copy-start.2 = (bf16[1,512,256]{2,1,0:T(8,128)(2,1)S(1)}, bf16[1,512,256]{2,1,0:T(8,128)(2,1)}, u32[]{:S(2)}) copy-start(bf16[1,512,256]{2,1,0:T(8,128)(2,1)} %param.16) | copy-start | bytes 786436
  59.4 26.7 %all-to-all-start.2 = ((bf16[16,8,2048]{2,1,0:T(8,128)(2,1)}), bf16[16,8,2048]{2,1,0:T(8,128)(2,1)S(1)}, u32[]{:S(2)}, u32[]{:S(2)}) async-start(bf16[16,8,2048]{2,1,0:T(8,128)(2,1)} %convert_element_type.57), calls=%async_computation.2 | async-start | bytes 1048576 | tf_op jit(solution)/shard_map/all_to_all | solution.py:194
  66.1 2.4 %copy-start.6 = (bf16[512,128]{1,0:T(8,128)(2,1)S(1)}, bf16[512,128]{1,0:T(8,128)(2,1)}, u32[]{:S(2)}) copy-start(bf16[512,128]{1,0:T(8,128)(2,1)} %get-tuple-element.228) | copy-start | bytes 393220 | tf_op jit(solution)/shard_map/while
  68.5 1.7 %copy-start.4 = (bf16[2,512,4,128]{3,1,2,0:T(8,128)(2,1)S(1)}, bf16[2,512,4,128]{3,1,2,0:T(8,128)(2,1)}, u32[]{:S(2)}) copy-start(bf16[2,512,4,128]{3,1,2,0:T(8,128)(2,1)} %get-tuple-element.216) | copy-start | bytes 3145732 | tf_op jit(solution)/shard_map/while
  72.4 1.0 %copy-start.5 = (bf16[2,512,4,128]{3,1,2,0:T(8,128)(2,1)}, bf16[2,512,4,128]{3,1,2,0:T(8,128)(2,1)S(1)}, u32[]{:S(2)}) copy-start(bf16[2,512,4,128]{3,1,2,0:T(8,128)(2,1)S(1)} %fusion.87) | copy-start | bytes 3145732 | tf_op jit(solution)/shard_map/while
  75.3 2.4 %copy-start.6 = (bf16[512,128]{1,0:T(8,128)(2,1)S(1)}, bf16[512,128]{1,0:T(8,128)(2,1)}, u32[]{:S(2)}) copy-start(bf16[512,128]{1,0:T(8,128)(2,1)} %get-tuple-element.228) | copy-start | bytes 393220 | tf_op jit(solution)/shard_map/while
  77.7 1.7 %copy-start.4 = (bf16[2,512,4,128]{3,1,2,0:T(8,128)(2,1)S(1)}, bf16[2,512,4,128]{3,1,2,0:T(8,128)(2,1)}, u32[]{:S(2)}) copy-start(bf16[2,512,4,128]{3,1,2,0:T(8,128)(2,1)} %get-tuple-element.216) | copy-start | bytes 3145732 | tf_op jit(solution)/shard_map/while
  81.6 1.0 %copy-start.5 = (bf16[2,512,4,128]{3,1,2,0:T(8,128)(2,1)}, bf16[2,512,4,128]{3,1,2,0:T(8,128)(2,1)S(1)}, u32[]{:S(2)}) copy-start(bf16[2,512,4,128]{3,1,2,0:T(8,128)(2,1)S(1)} %fusion.87) | copy-start | bytes 3145732 | tf_op jit(solution)/shard_map/while
where the time goes:
time: 89.1 us; the launch traced here: 88.5 us
  local copies, waits for them, and re-layouts  22.4 us (25%)
  matrix products  19.5 us (22%)
  starting transfers between devices  18.1 us (20%)
  waiting for transfers between devices  14.8 us (17%)
  other arithmetic  12.4 us (14%)
  between operations  1.03 us (1%)
    all_to_all x1, waiting for transfers between devices, shards(): lax.all_to_all(sending, 'pool', split_axis=0, concat_axis=0, tiled=True)  14.8 us
    all_to_all x1, starting transfers between devices, shards(): lax.all_to_all(outgoing, 'pool', split_axis=0, concat_axis=0, tiled=True)  7.36 us
    all_to_all x1, starting transfers between devices, shards(): lax.all_to_all(sending, 'pool', split_axis=0, concat_axis=0, tiled=True)  6.01 us
    all_to_all x1, starting transfers between devices, shards(): lax.all_to_all(answers.reshape(device_count, slot_cap, -1), 'pool', split...  4.78 us
    reduce_sum x2, other arithmetic, one_block(): jnp.sum(fresh_exp, axis=-1, keepdims=True)  4.75 us
    dot_general x1, matrix products, decode_attend(): jnp.einsum('skqd,sktd->skqt', queries, cache_slots[..., :head_dim], prefe...  4.62 us
    dot_general x2, matrix products, one_block(): jnp.einsum('hts,sd->thd', fresh_weights, new_kv[:, head_dim:], preferred_...  4.33 us
    gather x1, local copies, waits for them, and re-layouts, shards(): payload[row_index, member_index].reshape(device_count, slot_cap, -1)  3.6 us
  transfers between devices with their start and end apart: 3, of which 1 were waited for; matrix products, arithmetic and copies ran while one was open for 38% of the time, Pallas kernels for 0%

commit v1 on v0

v1 whole, which is shorter than its diff:
```python
import functools

import jax
import jax.numpy as jnp
from jax import lax
from jax.experimental import pallas as pl
from jax.experimental.pallas import tpu as pltpu
from jax.sharding import PartitionSpec as P

PGRP = 8
DGRP = 4
PCAP = 2
LANES = 128
MASKED = -1e30
LOG2E = 1.4426950408889634


def up16(n):
    return -(-n // 16) * 16


def any_spec():
    return pl.BlockSpec(memory_space=pl.ANY)


def smem_spec():
    return pl.BlockSpec(memory_space=pltpu.SMEM)


def vmem_spec():
    return pl.BlockSpec(memory_space=pltpu.VMEM)


def pack_kernel(
    layout, table, count, groups, pool, q, kv, out, rows_scr, group_fill, sems
):
    blk, cap, head_rows, own_rows, q_start, own_start = layout
    blocks_here = pool.shape[0]
    group_count, most_blocks = table.shape
    decode_groups = out.shape[0] // DGRP
    row_count = q.shape[0]
    head_total = q.shape[1] // LANES
    device = lax.axis_index("pool")
    first_block = device * blocks_here
    copies = []
    for g in range(group_count):

        def scan_table(j, carry):
            seen, chosen = carry
            entry = table[g, j]
            mine = (entry >= first_block) & (entry < first_block + blocks_here) & (j < count[g])
            chosen = tuple(
                jnp.where(mine & (seen == k), entry - first_block, chosen[k]) for k in range(PCAP)
            )
            return seen + mine.astype(jnp.int32), chosen

        start = (jnp.int32(0), tuple(jnp.int32(0) for _ in range(PCAP)))
        _, chosen = lax.fori_loop(0, most_blocks, scan_table, start, unroll=8)
        for k in range(PCAP):
            for part in range(2):
                copy = pltpu.make_async_copy(
                    pool.at[chosen[k], :, :, pl.ds(part * LANES, LANES)],
                    out.at[pl.ds(g * PGRP, PGRP), pl.ds((k * 2 + part) * blk, blk), :],
                    sems.at[(g * PCAP + k) * 2 + part],
                )
                copy.start()
                copies.append(copy)
    for a in range(decode_groups):
        group_fill[a] = 0
    for h in range(head_total):
        rows_scr[pl.ds(h, row_count, stride=head_total), :] = q[
            :, h * LANES : (h + 1) * LANES
        ].astype(jnp.float32)
    slot_axis = lax.broadcasted_iota(jnp.int32, (decode_groups * cap, row_count), 0)
    row_axis = lax.broadcasted_iota(jnp.int32, (decode_groups * cap, row_count), 1)
    slot_of_row = jnp.full((decode_groups * cap, row_count), -1, jnp.int32)
    for i in range(row_count):
        a = groups[device * row_count + i]
        c = group_fill[a]
        group_fill[a] = c + 1
        slot_of_row = jnp.where(row_axis == i, a * cap + c, slot_of_row)
        for m in range(DGRP):
            first = i * head_total + m * head_rows
            out[a * DGRP + m, pl.ds(q_start + pl.multiple_of(c * head_rows, 16), head_rows), :] = (
                rows_scr[first : first + head_rows, :].astype(out.dtype)
            )
    pick = (slot_of_row == slot_axis).astype(jnp.bfloat16)
    own = jnp.dot(pick, kv[...], preferred_element_type=jnp.float32)
    pair_count = kv.shape[1] // (2 * LANES * DGRP)
    blank = jnp.zeros((own_rows - pair_count * cap, LANES), jnp.float32)
    for a in range(decode_groups):
        for m in range(DGRP):
            for part in range(2):
                pieces = [
                    own[
                        a * cap : (a + 1) * cap,
                        ((m * pair_count + k) * 2 + part) * LANES : ((m * pair_count + k) * 2 + part + 1) * LANES,
                    ]
                    for k in range(pair_count)
                ]
                if blank.shape[0]:
                    pieces.append(blank)
                out[
                    a * DGRP + m,
                    own_start + part * own_rows : own_start + (part + 1) * own_rows,
                    :,
                ] = jnp.concatenate(pieces, axis=0).astype(out.dtype)
    for copy in copies:
        copy.wait()


def plan_kernel(cap, step, owners, table, count, groups, lengths, slot_len, listed, prefix_held):
    device = lax.axis_index("pool")
    home_count = owners
    row_count = groups.shape[0] // home_count
    group_id = device // DGRP
    prefill_id = device // PGRP
    blocks_here = listed.shape[0]
    most_blocks = table.shape[1]
    chunk = min(cap, step)

    def one_owner(o, carry):
        prefix_held[o] = 0
        return carry

    lax.fori_loop(0, owners, one_owner, 0)
    pool_blocks = prefix_held.shape[0] // owners

    def one_entry(j, carry):
        o = table[prefill_id, j] // pool_blocks
        prefix_held[o] = prefix_held[o] + 1
        return carry

    lax.fori_loop(0, jnp.minimum(count[prefill_id], most_blocks), one_entry, 0)

    def one_home(s, filled):
        for c in range(cap):
            slot_len[s * cap + c] = 0
        here = jnp.int32(0)
        for i in range(row_count):
            row = s * row_count + i
            mine = groups[row] == group_id
            place = s * cap + jnp.minimum(here, cap - 1)
            slot_len[place] = jnp.where(mine, lengths[row], slot_len[place])
            here = here + mine.astype(jnp.int32)
        for b in range(cap // chunk):
            listed[1 + jnp.minimum(filled, blocks_here - 2)] = s * (cap // chunk) + b
            filled = filled + (here > b * chunk).astype(jnp.int32)
        return filled

    listed[0] = lax.fori_loop(0, home_count, one_home, jnp.int32(0))


def decode_kernel(layout, chunk, width, listed, slot_len, recv, cache, out, held, sems):
    blk, cap, head_rows, own_rows, q_start, own_start = layout
    pair_count, positions = cache.shape[1], cache.shape[2]
    per_home = cap // chunk
    key_count = pair_count * positions
    query_heads = head_rows // pair_count
    live = listed[0]
    scale = LANES ** (-0.5)

    def fetch(i):
        return pltpu.make_async_copy(
            cache.at[pl.ds(listed[1 + i] * chunk, chunk)], held.at[i], sems.at[i]
        )

    def begin(i, carry):
        fetch(i).start()
        return carry

    lax.fori_loop(0, live, begin, 0)
    rows = chunk * head_rows
    row_pair = (
        lax.broadcasted_iota(jnp.int32, (chunk, head_rows, key_count), 1) // query_heads
    )
    key_axis = lax.broadcasted_iota(jnp.int32, (chunk, head_rows, key_count), 2)
    key_slot = lax.broadcasted_iota(jnp.int32, (chunk, head_rows, key_count), 0)
    pos = jnp.where(key_axis // positions == row_pair, key_axis % positions, positions)
    own_axis = lax.broadcasted_iota(jnp.int32, (rows, own_rows), 1)
    own_row = lax.broadcasted_iota(jnp.int32, (rows, own_rows), 0)
    own_want = ((own_row % head_rows) // query_heads) * cap + own_row // head_rows

    def one(i):
        block = listed[1 + i]
        home = block // per_home
        first = (block % per_home) * chunk
        kv = held[i]
        keys = kv[..., :LANES].reshape(chunk, key_count, LANES)
        values = kv[..., LANES:].reshape(chunk, key_count, LANES)
        place = pl.multiple_of(first * head_rows, 16)
        q = recv[home, pl.ds(q_start + place, rows), :]
        own_keys = recv[home, own_start : own_start + own_rows, :]
        own_values = recv[home, own_start + own_rows : own_start + 2 * own_rows, :]
        scores = jnp.einsum(
            "jqd,jkd->jqk",
            q.reshape(chunk, head_rows, LANES),
            keys,
            preferred_element_type=jnp.float32,
        )
        length = jnp.zeros_like(pos)
        for j in range(chunk):
            length = jnp.where(key_slot == j, slot_len[block * chunk + j], length)
        scores = jnp.where(pos < length, scores, MASKED)
        own_scores = lax.dot_general(
            q, own_keys, (((1,), (1,)), ((), ())), preferred_element_type=jnp.float32
        )
        own_hit = own_axis == own_want + first
        own_score = jnp.sum(jnp.where(own_hit, own_scores, 0.0), axis=1, keepdims=True)
        own_score3 = own_score.reshape(chunk, head_rows, 1)
        top = jnp.maximum(jnp.max(scores, axis=2, keepdims=True), own_score3)
        weights = jnp.exp2((scores - top) * (scale * LOG2E))
        own_weight = jnp.exp2((own_score3 - top) * (scale * LOG2E))
        total = jnp.sum(weights, axis=2, keepdims=True) + own_weight
        mixed = jnp.einsum(
            "jqk,jkd->jqd",
            weights.astype(jnp.bfloat16),
            values,
            preferred_element_type=jnp.float32,
        )
        own_part = jnp.where(own_hit, own_weight.reshape(rows, 1), 0.0).astype(jnp.bfloat16)
        mixed = mixed.reshape(rows, LANES) + jnp.dot(
            own_part, own_values, preferred_element_type=jnp.float32
        )
        answer = mixed / total.reshape(rows, 1)
        out[home, pl.ds(place, rows), :] = answer.astype(out.dtype)

    def several(t, carry):
        ids = [jnp.minimum(t * width + w, live - 1) for w in range(width)]
        for w in range(width):

            @pl.when(t * width + w < live)
            def _():
                fetch(t * width + w).wait()

        for i in ids:
            one(i)
        return carry

    lax.fori_loop(0, (live + width - 1) // width, several, 0)


def prefill_kernel(layout, tile, prefix_held, recv, q, new_kv, out, keys, values, bias):
    blk = layout[0]
    owners = recv.shape[0]
    prefix = owners * PCAP * blk
    token_count = new_kv.shape[0]
    scale = LANES ** (-0.5) * LOG2E

    @pl.when(pl.program_id(0) == 0)
    def _():
        lane_block = lax.broadcasted_iota(jnp.int32, (8, prefix), 1) // blk
        hide = jnp.zeros((8, prefix), jnp.float32)
        for o in range(owners):
            for k in range(PCAP):
                place = (o * PCAP + k) * blk
                keys[place : place + blk, :] = recv[o, (k * 2) * blk : (k * 2 + 1) * blk, :]
                values[place : place + blk, :] = recv[o, (k * 2 + 1) * blk : (k * 2 + 2) * blk, :]
                gone = jnp.where(prefix_held[o] > k, 0.0, MASKED)
                hide = jnp.where(lane_block == o * PCAP + k, gone, hide)
        bias[...] = hide
        keys[prefix:, :] = new_kv[:, :LANES]
        values[prefix:, :] = new_kv[:, LANES:]

    for t in range(token_count // tile):
        width = prefix + (t + 1) * tile
        block = q[t * tile : (t + 1) * tile, :]
        scores = lax.dot_general(
            block, keys[:width, :], (((1,), (1,)), ((), ())), preferred_element_type=jnp.float32
        )
        causal = lax.broadcasted_iota(jnp.int32, (tile, tile), 0) >= lax.broadcasted_iota(
            jnp.int32, (tile, tile), 1
        )
        pieces = [scores[:, :prefix] + bias[0:1, :]]
        if t:
            pieces.append(scores[:, prefix : width - tile])
        pieces.append(jnp.where(causal, scores[:, width - tile :], MASKED))
        scores = jnp.concatenate(pieces, axis=1)
        top = jnp.max(scores, axis=1, keepdims=True)
        weights = jnp.exp2((scores - top) * scale)
        total = jnp.sum(weights, axis=1, keepdims=True)
        mixed = jnp.dot(
            weights.astype(jnp.bfloat16), values[:width, :], preferred_element_type=jnp.float32
        )
        out[t * tile : (t + 1) * tile, :] = (mixed / total).astype(out.dtype)


def unpack_kernel(cap, head_rows, groups, back, out, rows_scr, group_fill):
    device = lax.axis_index("pool")
    row_count = out.shape[0]
    head_total = out.shape[1] // LANES
    for a in range(back.shape[0] // DGRP):
        group_fill[a] = 0
    for i in range(row_count):
        a = groups[device * row_count + i]
        c = group_fill[a]
        group_fill[a] = c + 1
        for m in range(DGRP):
            first = i * head_total + m * head_rows
            rows_scr[first : first + head_rows, :] = back[
                a * DGRP + m, pl.ds(pl.multiple_of(c * head_rows, 16), head_rows), :
            ].astype(jnp.float32)
    for h in range(head_total):
        out[:, h * LANES : (h + 1) * LANES] = rows_scr[
            pl.ds(h, row_count, stride=head_total), :
        ].astype(out.dtype)


def shards(
    pool_kv,
    prefix_table,
    prefix_count,
    prefill_q,
    prefill_new_kv,
    decode_q,
    decode_new,
    decode_cache,
    decode_group,
    cached_len,
):
    devices = lax.axis_size("pool")
    blk = pool_kv.shape[2]
    row_count, q_width = decode_q.shape
    cap = decode_cache.shape[1] // devices
    decode_groups = devices // DGRP
    pair_count = decode_cache.shape[2]
    head_rows = q_width // LANES // DGRP
    own_rows = up16(pair_count * cap)
    q_start = PCAP * 2 * blk
    own_start = q_start + cap * head_rows
    message_rows = own_start + 2 * own_rows
    layout = (blk, cap, head_rows, own_rows, q_start, own_start)
    groups = decode_group.reshape(-1)
    prefill_groups = prefix_table.shape[0]
    big = pltpu.CompilerParams(vmem_limit_bytes=40 * 2**20)

    sending = pl.pallas_call(
        functools.partial(pack_kernel, layout),
        out_shape=jax.ShapeDtypeStruct((devices, message_rows, LANES), jnp.bfloat16),
        in_specs=[smem_spec(), smem_spec(), smem_spec(), any_spec(), vmem_spec(), vmem_spec()],
        out_specs=vmem_spec(),
        scratch_shapes=[
            pltpu.VMEM((row_count * q_width // LANES, LANES), jnp.float32),
            pltpu.SMEM((decode_groups,), jnp.int32),
            pltpu.SemaphoreType.DMA((prefill_groups * PCAP * 2,)),
        ],
        compiler_params=big,
        name="pack",
    )(prefix_table, prefix_count, groups, pool_kv, decode_q, decode_new)

    received = lax.all_to_all(sending, "pool", split_axis=0, concat_axis=0, tiled=True)

    chunk = min(cap, 4)
    width = 4
    block_count = devices * cap // chunk
    slot_len, listed, prefix_held = pl.pallas_call(
        functools.partial(plan_kernel, cap, chunk, devices),
        out_shape=(
            jax.ShapeDtypeStruct((devices * cap,), jnp.int32),
            jax.ShapeDtypeStruct((block_count + 2,), jnp.int32),
            jax.ShapeDtypeStruct((devices * pool_kv.shape[0],), jnp.int32),
        ),
        in_specs=[smem_spec()] * 4,
        out_specs=(smem_spec(),) * 3,
        cost_estimate=pl.CostEstimate(flops=1000000, bytes_accessed=4000000, transcendentals=0),
        name="plan",
    )(prefix_table, prefix_count, groups, cached_len)

    answers = pl.pallas_call(
        functools.partial(decode_kernel, layout, chunk, width),
        out_shape=jax.ShapeDtypeStruct((devices, cap * head_rows, LANES), jnp.bfloat16),
        in_specs=[smem_spec(), smem_spec(), vmem_spec(), any_spec()],
        out_specs=vmem_spec(),
        scratch_shapes=[
            pltpu.VMEM((block_count, chunk) + decode_cache.shape[2:], jnp.bfloat16),
            pltpu.SemaphoreType.DMA((block_count,)),
        ],
        compiler_params=big,
        cost_estimate=pl.CostEstimate(
            flops=500000000, bytes_accessed=8000000, transcendentals=1000000
        ),
        name="decode",
    )(listed, slot_len, received, decode_cache[0])

    back = lax.all_to_all(answers, "pool", split_axis=0, concat_axis=0, tiled=True)

    token_count, fill_width = prefill_q.shape[1:]
    prefix = devices * PCAP * blk
    head_count = fill_width // LANES
    prefix_held, received, _ = lax.optimization_barrier((prefix_held, received, answers))
    prefill_out = pl.pallas_call(
        functools.partial(prefill_kernel, layout, min(256, token_count)),
        grid=(head_count,),
        out_shape=jax.ShapeDtypeStruct((token_count, fill_width), jnp.bfloat16),
        in_specs=[
            smem_spec(),
            pl.BlockSpec((devices, PCAP * 2 * blk, LANES), lambda u: (0, 0, 0)),
            pl.BlockSpec((token_count, LANES), lambda u: (0, u)),
            pl.BlockSpec(prefill_new_kv.shape[1:], lambda u: (0, 0)),
        ],
        out_specs=pl.BlockSpec((token_count, LANES), lambda u: (0, u)),
        scratch_shapes=[
            pltpu.VMEM((prefix + token_count, LANES), jnp.bfloat16),
            pltpu.VMEM((prefix + token_count, LANES), jnp.bfloat16),
            pltpu.VMEM((8, prefix), jnp.float32),
        ],
        compiler_params=big,
        cost_estimate=pl.CostEstimate(
            flops=2 * 2 * token_count * fill_width * (prefix + token_count // 2),
            bytes_accessed=3000000,
            transcendentals=token_count * head_count * (prefix + token_count // 2),
        ),
        name="prefill",
    )(prefix_held, received, prefill_q[0], prefill_new_kv[0])

    decode_out = pl.pallas_call(
        functools.partial(unpack_kernel, cap, head_rows),
        out_shape=jax.ShapeDtypeStruct((row_count, q_width), jnp.bfloat16),
        in_specs=[smem_spec(), vmem_spec()],
        out_specs=vmem_spec(),
        scratch_shapes=[
            pltpu.VMEM((row_count * q_width // LANES, LANES), jnp.float32),
            pltpu.SMEM((decode_groups,), jnp.int32),
        ],
        name="unpack",
    )(groups, back)
    return (prefill_out[None], decode_out)


def solution(mesh):
    in_specs = (
        P(("rep", "pool"), None, None, None),
        P("rep", None),
        P("rep"),
        P(("rep", "pool"), None, None),
        P(("rep", "pool"), None, None),
        P(("rep", "pool"), None),
        P(("rep", "pool"), None),
        P(("rep", "pool"), None, None, None, None),
        P("rep", None),
        P("rep"),
    )
    out_specs = (P(("rep", "pool"), None, None), P(("rep", "pool"), None))
    return jax.shard_map(shards, mesh=mesh, in_specs=in_specs, out_specs=out_specs, check_vma=False)
```

time: 89.1 us -> 77.9 us (0.87)
  Pallas kernels: 0 us -> 25.6 us
  matrix products: 19.5 us -> 0 us
  other arithmetic: 12.4 us -> 0 us
  local copies, waits for them, and re-layouts: 22.4 us -> 10.2 us
  waiting for transfers between devices: 14.8 us -> 21.6 us
  starting transfers between devices: 18.1 us -> 19.2 us
    pallas_call x0 -> x5, Pallas kernels: none -> 25.6 us  [the longest x1 10.8 us: shards(): pl.pallas_call(functools.partial(prefill_kernel, layout, min(256, token_c...]
    dot_general x11 -> x0, matrix products: 19.5 us -> none  [the longest x1 4.62 us: decode_attend(): jnp.einsum('skqd,sktd->skqt', queries, cache_slots[..., :head_dim], prefe...]
    unnamed x15 -> x26, local copies, waits for them, and re-layouts: 0.74 us -> 10.2 us
    gather x5 -> x0, local copies, waits for them, and re-layouts: 7.73 us -> none  [the longest x1 3.6 us: shards(): payload[row_index, member_index].reshape(device_count, slot_cap, -1)]
    reduce_sum x8 -> x0, other arithmetic: 6.51 us -> none  [the longest x2 4.75 us: one_block(): jnp.sum(fresh_exp, axis=-1, keepdims=True)]
    all_to_all x2 -> x1, waiting for transfers between devices: 0.01 us -> 3.65 us  [shards(): lax.all_to_all(answers, 'pool', split_axis=0, concat_axis=0, tiled=True)]
    all_to_all x1, waiting for transfers between devices: 14.8 us -> 17.9 us  [shards(): lax.all_to_all(sending, 'pool', split_axis=0, concat_axis=0, tiled=True)]
    reshape x4 -> x0, local copies, waits for them, and re-layouts: 2.96 us -> none  [the longest x1 1.14 us: shards(): decode_q.reshape(row_count, DGRP, -1)]
  transfers between devices with their start and end apart: 3 -> 2, of which waited for: 1 -> 2; matrix products, arithmetic and copies ran while one was open for 38% -> 0% of each run, Pallas kernels for 0% -> 18%
where the time goes in v1:
time: 77.9 us; the launch traced here: 77.3 us
  Pallas kernels  25.6 us (33%)
  waiting for transfers between devices  21.6 us (28%)
  starting transfers between devices  19.2 us (25%)
  local copies, waits for them, and re-layouts  10.2 us (13%)
    all_to_all x1, waiting for transfers between devices, shards(): lax.all_to_all(sending, 'pool', split_axis=0, concat_axis=0, tiled=True)  17.9 us
    all_to_all x1, starting transfers between devices, shards(): lax.all_to_all(answers, 'pool', split_axis=0, concat_axis=0, tiled=True)  11.9 us
    pallas_call x1, Pallas kernels, shards(): pl.pallas_call(functools.partial(prefill_kernel, layout, min(256, token_c...  10.8 us
    unnamed x26, local copies, waits for them, and re-layouts  10.2 us
    all_to_all x1, starting transfers between devices, shards(): lax.all_to_all(sending, 'pool', split_axis=0, concat_axis=0, tiled=True)  7.37 us
    pallas_call x1, Pallas kernels, shards(): pl.pallas_call(functools.partial(decode_kernel, layout, chunk, width), ou...  7.31 us
    all_to_all x1, waiting for transfers between devices, shards(): lax.all_to_all(answers, 'pool', split_axis=0, concat_axis=0, tiled=True)  3.65 us
    pallas_call x1, Pallas kernels, shards(): pl.pallas_call(functools.partial(plan_kernel, cap, chunk, devices), out_s...  2.87 us
  transfers between devices with their start and end apart: 2, of which 2 were waited for; matrix products, arithmetic and copies ran while one was open for 0% of the time, Pallas kernels for 18%

profile of v1, /device:TPU:0, one launch (start us, length us, event | category | flops | bytes accessed | tf_op | source)
XLA Modules:
  0.0 77.3 jit_solution(3606016967343178197)
XLA Ops:
  0.6 0.0 copy-start.1
  0.6 0.9 %copy-done.1 = bf16[4,8,16,256]{3,2,1,0:T(8,128)(2,1)S(1)} copy-done((bf16[4,8,16,256]{3,2,1,0:T(8,128)(2,1)S(1)}, bf16[4,8,16,256]{3,2,1,0:T(8,128)(2,1)}, u32[]{:S(2)}) %copy-start.1) | copy-done | bytes 262168
  1.6 0.0 copy-start.2
  1.6 0.9 %copy-done.2 = bf16[16,8192]{1,0:T(8,128)(2,1)S(1)} copy-done((bf16[16,8192]{1,0:T(8,128)(2,1)S(1)}, bf16[16,8192]{1,0:T(8,128)(2,1)}, u32[]{:S(2)}) %copy-start.2) | copy-done | bytes 262168
  2.5 0.0 copy-start.3
  2.5 0.8 %copy-done.3 = bf16[16,2048]{1,0:T(8,128)(2,1)S(1)} copy-done((bf16[16,2048]{1,0:T(8,128)(2,1)S(1)}, bf16[16,2048]{1,0:T(8,128)(2,1)}, u32[]{:S(2)}) %copy-start.3) | copy-done | bytes 65560
  3.4 0.0 copy-start.4
  3.4 0.7 copy-done.4
  4.1 0.0 copy-start.5
  4.1 0.7 copy-done.5
  4.7 0.0 copy-start.6
  4.7 0.7 copy-done.6
  5.4 0.0 copy-start.9
  5.4 0.0 copy-start.10
  5.4 2.5 %pack.1 = bf16[16,224,128]{2,1,0:T(8,128)(2,1)} custom-call(s32[2,32]{1,0:T(2,128)S(1)} %copy-done.5, s32[2]{0:T(128)S(1)} %copy-done.6, s32[256]{0:T(256)S(1)} %bitcast.8, bf16[4,8,16,256]{3,2,1,0:T(8,128)(2,1)S(1)} %copy-done.1, bf16[16,8192]{1,0:T(8,128)(2,1)S(1)} %copy-done.2, bf16[16,2048]{1,0:T(8,128)(2,1)S(1)} %copy-done.3), custom_call_target="tpu_custom_call" | custom-call | tf_op jit(solution)/shard_map/pack/pallas_call | solution.py:337
  7.9 7.4 %all-to-all-start = ((bf16[16,224,128]{2,1,0:T(8,128)(2,1)}), bf16[16,224,128]{2,1,0:T(8,128)(2,1)S(1)}, u32[]{:S(2)}, u32[]{:S(2)}) async-start(bf16[16,224,128]{2,1,0:T(8,128)(2,1)} %pack.1), calls=%async_computation | async-start | bytes 1835008 | tf_op jit(solution)/shard_map/all_to_all | solution.py:351
  15.3 2.9 %plan.1 = (s32[128]{0:T(128)}, s32[34]{0:T(128)}, s32[64]{0:T(128)}) custom-call(s32[2,32]{1,0:T(2,128)} %table.3, s32[2]{0:T(128)} %count.3, s32[256]{0:T(256)} %bitcast.6, s32[256]{0:T(256)} %lengths.1), custom_call_target="tpu_custom_call" | custom-call | flops 1000000 | bytes 4000000 | tf_op jit(solution)/shard_map/plan/pallas_call | solution.py:356
  18.2 0.0 copy-start.11
  18.2 17.9 %all-to-all-done.recv = bf16[16,224,128]{2,1,0:T(8,128)(2,1)S(1)} async-done(((bf16[16,224,128]{2,1,0:T(8,128)(2,1)}), bf16[16,224,128]{2,1,0:T(8,128)(2,1)S(1)}, u32[]{:S(2)}, u32[]{:S(2)}) %all-to-all-start) | async-done | bytes 917536 | tf_op jit(solution)/shard_map/all_to_all | solution.py:351
  36.1 0.0 copy-start
  36.1 3.4 %copy-done = bf16[1,128,2,64,256]{4,3,2,1,0:T(8,128)(2,1)S(1)} copy-done((bf16[1,128,2,64,256]{4,3,2,1,0:T(8,128)(2,1)S(1)}, bf16[1,128,2,64,256]{4,3,2,1,0:T(8,128)(2,1)}, u32[]{:S(2)}) %copy-start) | copy-done | bytes 8388632
  39.5 0.0 copy-start.7
  39.5 0.7 copy-done.7
  40.2 0.0 copy-start.8
  40.2 0.6 copy-done.8
  40.7 7.3 %decode.1 = bf16[16,128,128]{2,1,0:T(8,128)(2,1)} custom-call(s32[34]{0:T(128)S(1)} %copy-done.8, s32[128]{0:T(128)S(1)} %copy-done.7, bf16[16,224,128]{2,1,0:T(8,128)(2,1)S(1)} %all-to-all-done.recv, bf16[128,2,64,256]{3,2,1,0:T(8,128)(2,1)S(1)} %bitcast.5), custom_call_target="tpu_custom_call" | custom-call | flops 500000000 | bytes 8000000 | tf_op jit(solution)/shard_map/decode/pallas_call | solution.py:369
  48.1 11.9 %all-to-all-start.1 = ((bf16[16,128,128]{2,1,0:T(8,128)(2,1)}), bf16[16,128,128]{2,1,0:T(8,128)(2,1)S(1)}, u32[]{:S(2)}, u32[]{:S(2)}) async-start(bf16[16,128,128]{2,1,0:T(8,128)(2,1)} %decode.1), calls=%async_computation.1 | async-start | bytes 1048576 | tf_op jit(solution)/shard_map/all_to_all | solution.py:385
  59.9 0.0 copy-done.9
  59.9 0.0 copy-done.10
  59.9 0.0 copy-done.11
  59.9 10.8 %prefill.1 = bf16[512,1024]{1,0:T(8,128)(2,1)} custom-call(s32[64]{0:T(128)S(1)} %copy-done.11, bf16[16,224,128]{2,1,0:T(8,128)(2,1)S(1)} %all-to-all-done.recv, bf16[512,1024]{1,0:T(8,128)(2,1)S(1)} %bitcast.9, bf16[512,256]{1,0:T(8,128)(2,1)S(1)} %bitcast.10), custom_call_target="tpu_custom_call" | custom-call | flops 1610612736 | bytes 3000000 | tf_op jit(solution)/shard_map/prefill/pallas_call | solution.py:391
  70.7 3.7 %all-to-all-done.1.back = bf16[16,128,128]{2,1,0:T(8,128)(2,1)S(1)} async-done(((bf16[16,128,128]{2,1,0:T(8,128)(2,1)}), bf16[16,128,128]{2,1,0:T(8,128)(2,1)S(1)}, u32[]{:S(2)}, u32[]{:S(2)}) %all-to-all-start.1) | async-done | bytes 524320 | tf_op jit(solution)/shard_map/all_to_all | solution.py:385
  74.4 0.0 copy-start.12
  74.4 0.8 %copy-done.12 = bf16[16,128,128]{2,1,0:T(8,128)(2,1)} copy-done((bf16[16,128,128]{2,1,0:T(8,128)(2,1)}, bf16[16,128,128]{2,1,0:T(8,128)(2,1)S(1)}, u32[]{:S(2)}) %copy-start.12) | copy-done | bytes 524312
  75.2 2.1 %unpack.1 = bf16[16,8192]{1,0:T(8,128)(2,1)} custom-call(s32[256]{0:T(256)} %bitcast.7, bf16[16,128,128]{2,1,0:T(8,128)(2,1)} %copy-done.12), custom_call_target="tpu_custom_call" | custom-call | tf_op jit(solution)/shard_map/unpack/pallas_call | solution.py:416
Async XLA Ops:
  0.6 1.0 %copy-start.1 = (bf16[4,8,16,256]{3,2,1,0:T(8,128)(2,1)S(1)}, bf16[4,8,16,256]{3,2,1,0:T(8,128)(2,1)}, u32[]{:S(2)}) copy-start(bf16[4,8,16,256]{3,2,1,0:T(8,128)(2,1)} %pool.1) | copy-start | bytes 786436
  1.6 0.9 %copy-start.2 = (bf16[16,8192]{1,0:T(8,128)(2,1)S(1)}, bf16[16,8192]{1,0:T(8,128)(2,1)}, u32[]{:S(2)}) copy-start(bf16[16,8192]{1,0:T(8,128)(2,1)} %q.1) | copy-start | bytes 786436
  2.5 0.8 %copy-start.3 = (bf16[16,2048]{1,0:T(8,128)(2,1)S(1)}, bf16[16,2048]{1,0:T(8,128)(2,1)}, u32[]{:S(2)}) copy-start(bf16[16,2048]{1,0:T(8,128)(2,1)} %kv.1) | copy-start | bytes 196612
  3.4 0.7 copy-start.4
  4.1 0.7 copy-start.5
  4.7 0.7 copy-start.6
  5.4 54.5 %copy-start.9 = (bf16[1,512,1024]{2,1,0:T(8,128)(2,1)S(1)}, bf16[1,512,1024]{2,1,0:T(8,128)(2,1)}, u32[]{:S(2)}) copy-start(bf16[1,512,1024]{2,1,0:T(8,128)(2,1)} %param.13) | copy-start | bytes 3145732
  5.4 54.5 %copy-start.10 = (bf16[1,512,256]{2,1,0:T(8,128)(2,1)S(1)}, bf16[1,512,256]{2,1,0:T(8,128)(2,1)}, u32[]{:S(2)}) copy-start(bf16[1,512,256]{2,1,0:T(8,128)(2,1)} %param.14) | copy-start | bytes 786436
  7.9 28.2 %all-to-all-start = ((bf16[16,224,128]{2,1,0:T(8,128)(2,1)}), bf16[16,224,128]{2,1,0:T(8,128)(2,1)S(1)}, u32[]{:S(2)}, u32[]{:S(2)}) async-start(bf16[16,224,128]{2,1,0:T(8,128)(2,1)} %pack.1), calls=%async_computation | async-start | bytes 1835008 | tf_op jit(solution)/shard_map/all_to_all | solution.py:351
  18.2 41.7 %copy-start.11 = (s32[64]{0:T(128)S(1)}, s32[64]{0:T(128)}, u32[]{:S(2)}) copy-start(s32[64]{0:T(128)} %get-tuple-element.10.prefix_held) | copy-start | bytes 772
  36.1 3.4 %copy-start = (bf16[1,128,2,64,256]{4,3,2,1,0:T(8,128)(2,1)S(1)}, bf16[1,128,2,64,256]{4,3,2,1,0:T(8,128)(2,1)}, u32[]{:S(2)}) copy-start(bf16[1,128,2,64,256]{4,3,2,1,0:T(8,128)(2,1)} %param.17) | copy-start | bytes 25165828
  39.5 0.7 copy-start.7
  40.2 0.6 copy-start.8
  48.1 26.3 %all-to-all-start.1 = ((bf16[16,128,128]{2,1,0:T(8,128)(2,1)}), bf16[16,128,128]{2,1,0:T(8,128)(2,1)S(1)}, u32[]{:S(2)}, u32[]{:S(2)}) async-start(bf16[16,128,128]{2,1,0:T(8,128)(2,1)} %decode.1), calls=%async_computation.1 | async-start | bytes 1048576 | tf_op jit(solution)/shard_map/all_to_all | solution.py:385
  74.4 0.8 %copy-start.12 = (bf16[16,128,128]{2,1,0:T(8,128)(2,1)}, bf16[16,128,128]{2,1,0:T(8,128)(2,1)S(1)}, u32[]{:S(2)}) copy-start(bf16[16,128,128]{2,1,0:T(8,128)(2,1)S(1)} %all-to-all-done.1.back) | copy-start | bytes 1572868
